TPU v7x, 512 devices: a whole 4x4x16 slice. The times are simulated.
512 devices in a mesh: coil: 16 (over z_lo, core), slab: 32 (over x, z_hi, y).
Axes of the slice: x: 4, y: 4, z: 16 (z_hi: 2, z_lo: 8; z = z_hi * 8 + z_lo), core: 2. Of those that a mesh axis runs over, the one named last changes fastest.
Arguments:
- kspace_data: bfloat16 [32, 2, 128, 128, 128], P('coil', None, None, 'slab'), may hold values from -4 to 4
- coil_maps: bfloat16 [32, 2, 128, 128, 128], P('coil', None, 'slab'), may hold values from -1.796875 to 1.796875
- sample_mask: int32 [32, 128, 128], P('coil', None, 'slab'), may hold values 0 or 1
- initial_image: float32 [2, 128, 128, 128], P(None, 'slab', 'coil'), may hold values from -6 to 6
Outputs:
- image: float32 [2, 128, 128, 128], P(None, 'slab', 'coil')
All inputs are finite; a program needn't handle non-finite values. No bound on the sum of `sample_mask` on one device may be relied on, other than what follows from the above.
Results may differ from a plain program's by a relative error of at most 0.0045.
Values may be sent and summed in bfloat16 or wider, within the bound.
No kernel may reach another device: no remote copies, remote signals or barrier semaphores. Data moves between devices by JAX's collectives and lax.ppermute only.
A program may use at most 64 MiB of HBM per device.

v0:
```python
import math
import jax
import jax.numpy as jnp
from jax import lax
from jax.sharding import PartitionSpec as P

NX = 128
NY = 128
NZ = 128
ITERS = 2
dual_step = 0.25
primal_step = 0.25
tv_weight = 0.5


def from_behind(block, axis, distance):
    devices = range(lax.axis_size(axis))
    route = [(i - distance, i) for i in devices if i - distance in devices]
    return lax.ppermute(block, axis, route)


def in_blocks(shard, dim, size):
    before, after = (shard.shape[:dim], shard.shape[dim + 1 :])
    return jnp.moveaxis(shard.reshape(*before, size, -1, *after), dim, 0)


def sum_at_owner(shard, axis, dim):
    tiles = in_blocks(shard, dim, lax.axis_size(axis))
    arrived = lax.all_to_all(tiles, axis, split_axis=0, concat_axis=0, tiled=True)
    return arrived.sum(axis=0)


def dft_table(length, inverse):
    counter = jnp.arange(length, dtype=jnp.int32)
    product = counter[:, None] * counter[None, :] % length
    phase = 2.0 * math.pi / length * product.astype(jnp.float32)
    scale = 1.0 / math.sqrt(length)
    real_part = jnp.cos(phase) * scale
    imag_part = jnp.sin(phase) * scale
    if not inverse:
        imag_part = -imag_part
    table = jnp.stack([jnp.stack([real_part, imag_part]), jnp.stack([-imag_part, real_part])])
    return table.astype(jnp.bfloat16)


def data_term(guess, coil_maps, kspace_data, sample_mask, dual_data, tables):
    forward_x, forward_y, forward_z, inverse_x, inverse_y, inverse_z = tables
    maps_real = coil_maps[:, 0].astype(jnp.float32)
    maps_imag = coil_maps[:, 1].astype(jnp.float32)
    pieces = jnp.stack(
        [maps_real * guess[0] - maps_imag * guess[1], maps_real * guess[1] + maps_imag * guess[0]],
        1,
    ).astype(jnp.bfloat16)
    pieces = jnp.einsum(
        "ckzyx,kjxw->cjzyw", pieces, forward_x, preferred_element_type=jnp.float32
    ).astype(jnp.bfloat16)
    pieces = jnp.einsum(
        "ckzyx,kjyv->cjzvx", pieces, forward_y, preferred_element_type=jnp.float32
    ).astype(jnp.bfloat16)
    spectrum = jnp.einsum(
        "ckzyx,kjzw->cjwyx",
        lax.all_to_all(pieces, "slab", split_axis=3, concat_axis=2, tiled=True),
        forward_z,
        preferred_element_type=jnp.float32,
    )
    sampled = sample_mask[:, None, :, :, None].astype(jnp.float32)
    dual_new = (
        dual_data + dual_step * (sampled * (spectrum - kspace_data.astype(jnp.float32)))
    ) / (1.0 + dual_step)
    back_field = jnp.einsum(
        "ckzyx,kjzw->cjwyx",
        dual_new.astype(jnp.bfloat16),
        inverse_z,
        preferred_element_type=jnp.float32,
    ).astype(jnp.bfloat16)
    back_field = jnp.einsum(
        "ckzyx,kjyv->cjzvx",
        lax.all_to_all(back_field, "slab", split_axis=2, concat_axis=3, tiled=True),
        inverse_y,
        preferred_element_type=jnp.float32,
    ).astype(jnp.bfloat16)
    back_field = jnp.einsum(
        "ckzyx,kjxw->cjzyw", back_field, inverse_x, preferred_element_type=jnp.float32
    )
    real_sum = jnp.sum(maps_real * back_field[:, 0] + maps_imag * back_field[:, 1], 0)
    imag_sum = jnp.sum(maps_real * back_field[:, 1] - maps_imag * back_field[:, 0], 0)
    return (jnp.stack([real_sum, imag_sum]), dual_new)


def tv_update(guess, duals):
    planes = guess.shape[1]
    plane_pos = lax.axis_index("slab") * planes + lax.broadcasted_iota(
        jnp.int32, (1, planes, 1, 1), 1
    )
    next_plane = from_behind(guess[:, :1], "slab", -1)
    ahead_z = jnp.concatenate([guess[:, 1:], next_plane], 1)
    grad_z = jnp.where(plane_pos < NZ - 1, ahead_z - guess, 0.0)
    grad_y = jnp.concatenate(
        [guess[:, :, 1:] - guess[:, :, :-1], jnp.zeros_like(guess[:, :, :1])], 2
    )
    grad_x = jnp.concatenate([guess[..., 1:] - guess[..., :-1], jnp.zeros_like(guess[..., :1])], 3)
    moved_z = duals[0] + dual_step * grad_z
    moved_y = duals[1] + dual_step * grad_y
    moved_x = duals[2] + dual_step * grad_x
    magnitude = jnp.sqrt(
        jnp.sum(moved_z * moved_z, 0)
        + jnp.sum(moved_y * moved_y, 0)
        + jnp.sum(moved_x * moved_x, 0)
    )
    factor = 1.0 / jnp.maximum(1.0, magnitude / tv_weight)
    dual_z = moved_z * factor
    dual_y = moved_y * factor
    dual_x = moved_x * factor
    prior_plane = from_behind(dual_z[:, -1:], "slab", 1)
    spread_z = jnp.concatenate([prior_plane, dual_z[:, :-1]], 1) - dual_z
    spread_y = jnp.concatenate([jnp.zeros_like(dual_y[:, :, :1]), dual_y[:, :, :-1]], 2) - dual_y
    spread_x = jnp.concatenate([jnp.zeros_like(dual_x[..., :1]), dual_x[..., :-1]], 3) - dual_x
    return ((dual_z, dual_y, dual_x), spread_z + spread_y + spread_x)


def on_device(kspace_data, coil_maps, sample_mask, initial_image):
    tables = (
        dft_table(NX, False),
        dft_table(NY, False),
        dft_table(NZ, False),
        dft_table(NX, True),
        dft_table(NY, True),
        dft_table(NZ, True),
    )
    dual_data = jnp.zeros(kspace_data.shape, jnp.float32)
    share_rows = initial_image.shape[2]
    current = initial_image
    guess = current
    duals = None
    for turn_index in range(ITERS):
        whole_guess = lax.all_gather(guess, "coil", axis=2, tiled=True)
        if duals is None:
            duals = (
                jnp.zeros_like(whole_guess),
                jnp.zeros_like(whole_guess),
                jnp.zeros_like(whole_guess),
            )
        data_grad, dual_data = data_term(
            whole_guess, coil_maps, kspace_data, sample_mask, dual_data, tables
        )
        data_grad = sum_at_owner(data_grad, "coil", 2)
        duals, spread = tv_update(whole_guess, duals)
        spread_share = lax.dynamic_slice_in_dim(
            spread, lax.axis_index("coil") * share_rows, share_rows, 2
        )
        updated = current - primal_step * (data_grad + spread_share)
        guess = 2.0 * updated - current
        current = updated
    return current


def solution(mesh):
    placed = (
        P("coil", None, None, "slab", None),
        P("coil", None, "slab", None, None),
        P("coil", None, "slab"),
        P(None, "slab", "coil", None),
    )
    return jax.shard_map(
        on_device,
        mesh=mesh,
        in_specs=placed,
        out_specs=P(None, "slab", "coil", None),
        check_vma=False,
    )
```

profile of v0, /device:TPU:130, one launch (start us, length us, event | category | flops | bytes accessed | tf_op | source)
XLA Modules:
  0.0 341.5 jit_solution(4469572003324194506)
XLA Ops:
  1.0 20.8 %all_gather.6 = f32[2,4,128,128]{3,2,1,0:T(8,128)S(1)} all-gather(f32[2,4,8,128]{3,2,1,0:T(8,128)S(1)} %copy-done.6), channel_id=1, replica_groups=mesh['coil'=16,'slab'=32] {'coil'}, dimensions={2}, use_global_device_ids=true | all-gather | bytes 557056 | tf_op jit(solution)/shard_map/all_gather | solution.py:136
  21.8 1.0 copy-done.2
  23.6 1.2 copy.77
  24.8 13.6 %all-to-all-start = ((bf16[2,2,4,128,128]{4,2,0,1,3:T(4,128)(2,1)}), bf16[2,2,4,128,128]{4,2,0,1,3:T(4,128)(2,1)S(1)}, u32[]{:S(2)}, u32[]{:S(2)}) async-start(bf16[2,2,4,128,128]{4,2,0,1,3:T(4,128)(2,1)} %copy.77), calls=%async_computation | async-start | bytes 1048576 | tf_op jit(solution)/shard_map/all_to_all | solution.py:62
  38.5 19.4 %all-to-all-done = bf16[2,2,4,128,128]{4,2,0,1,3:T(4,128)(2,1)S(1)} async-done(((bf16[2,2,4,128,128]{4,2,0,1,3:T(4,128)(2,1)}), bf16[2,2,4,128,128]{4,2,0,1,3:T(4,128)(2,1)S(1)}, u32[]{:S(2)}, u32[]{:S(2)}) %all-to-all-start) | async-done | bytes 524320 | tf_op jit(solution)/shard_map/all_to_all | solution.py:62
  58.2 0.8 copy-done.4
  58.9 1.3 fusion.105
  61.0 33.9 %all_to_all.82 = bf16[2,2,128,4,128]{4,3,0,1,2:T(4,128)(2,1)S(1)} all-to-all(bf16[2,2,128,4,128]{4,3,0,1,2:T(4,128)(2,1)S(1)} %copy.82), channel_id=1, replica_groups=mesh['coil'=16,'slab'=32] {'slab'}, dimensions={2} | all-to-all | bytes 1048576 | tf_op jit(solution)/shard_map/all_to_all | solution.py:78
  95.9 0.9 copy.92
  96.8 26.0 %all-to-all-start.2 = ((f32[16,2,4,8,128]{4,3,2,1,0:T(8,128)}), f32[16,2,4,8,128]{4,3,2,1,0:T(8,128)}, u32[]{:S(2)}, u32[]{:S(2)}) async-start(f32[16,2,4,8,128]{4,3,2,1,0:T(8,128)} %copy.92), calls=%async_computation.2 | async-start | bytes 1048576 | tf_op jit(solution)/shard_map/all_to_all | solution.py:29
  122.8 9.0 %collective-permute-start = (f32[2,1,128,128]{3,2,1,0:T(8,128)S(1)}, f32[2,1,128,128]{3,2,1,0:T(8,128)S(1)}, u32[]{:S(2)}, u32[]{:S(2)}) collective-permute-start(f32[2,1,128,128]{3,2,1,0:T(8,128)S(1)} %slice.135), channel_id=1, source_target_pairs={{1,0},{2,1},{3,2},{4,3},{5,4},{6,5},{7,6},{8,7},{9,8},{10,9},{11,1... | collective-permute-start | bytes 393224 | tf_op jit(solution)/shard_map/ppermute | solution.py:19
  132.3 23.6 %collective-permute-done = f32[2,1,128,128]{3,2,1,0:T(8,128)S(1)} collective-permute-done((f32[2,1,128,128]{3,2,1,0:T(8,128)S(1)}, f32[2,1,128,128]{3,2,1,0:T(8,128)S(1)}, u32[]{:S(2)}, u32[]{:S(2)}) %collective-permute-start) | collective-permute-done | bytes 131104 | tf_op jit(solution)/shard_map/ppermute | solution.py:19
  156.5 1.9 collective-permute-start.1
  158.5 1.1 reduce_sum.110
  159.6 18.0 %collective-permute-done.1 = f32[2,1,128,128]{3,2,1,0:T(8,128)S(1)} collective-permute-done((f32[2,1,128,128]{3,2,1,0:T(8,128)S(1)}, f32[2,1,128,128]{3,2,1,0:T(8,128)S(1)}, u32[]{:S(2)}, u32[]{:S(2)}) %collective-permute-start.1) | collective-permute-done | bytes 131104 | tf_op jit(solution)/shard_map/ppermute | solution.py:19
  177.6 15.8 %all_gather.7 = f32[2,4,128,128]{3,2,1,0:T(8,128)S(1)} all-gather(f32[2,4,8,128]{3,2,1,0:T(8,128)S(1)} %get-tuple-element.11), channel_id=1, replica_groups=mesh['coil'=16,'slab'=32] {'coil'}, dimensions={2}, use_global_device_ids=true | all-gather | bytes 557056 | tf_op jit(solution)/shard_map/all_gather | solution.py:136
  193.4 1.0 fusion.32
  194.4 2.4 fusion.18
  196.8 1.4 copy.94
  198.3 35.9 %all_to_all.83 = bf16[2,2,4,128,128]{4,2,0,1,3:T(4,128)(2,1)S(1)} all-to-all(bf16[2,2,4,128,128]{4,2,0,1,3:T(4,128)(2,1)S(1)} %copy.94), channel_id=1, replica_groups=mesh['coil'=16,'slab'=32] {'slab'}, dimensions={3} | all-to-all | bytes 1048576 | tf_op jit(solution)/shard_map/all_to_all | solution.py:62
  234.5 0.8 copy-done.5
  236.4 26.2 %all_to_all.84 = bf16[2,2,128,4,128]{4,3,0,1,2:T(4,128)(2,1)S(1)} all-to-all(bf16[2,2,128,4,128]{4,3,0,1,2:T(4,128)(2,1)S(1)} %copy.99), channel_id=1, replica_groups=mesh['coil'=16,'slab'=32] {'slab'}, dimensions={2} | all-to-all | bytes 1048576 | tf_op jit(solution)/shard_map/all_to_all | solution.py:78
  262.7 1.1 copy.100
  263.8 2.5 convolution_bitcast_fusion
  266.3 1.4 fusion.36
  267.8 0.9 copy.109
  268.7 18.8 %all-to-all-start.5 = ((f32[16,2,4,8,128]{4,3,2,1,0:T(8,128)}), f32[16,2,4,8,128]{4,3,2,1,0:T(8,128)}, u32[]{:S(2)}, u32[]{:S(2)}) async-start(f32[16,2,4,8,128]{4,3,2,1,0:T(8,128)} %copy.109), calls=%async_computation.5 | async-start | bytes 1048576 | tf_op jit(solution)/shard_map/all_to_all | solution.py:29
  287.5 10.7 %collective-permute-start.2 = (f32[2,1,128,128]{3,2,1,0:T(8,128)S(1)}, f32[2,1,128,128]{3,2,1,0:T(8,128)S(1)}, u32[]{:S(2)}, u32[]{:S(2)}) collective-permute-start(f32[2,1,128,128]{3,2,1,0:T(8,128)S(1)} %slice.149), channel_id=1, source_target_pairs={{1,0},{2,1},{3,2},{4,3},{5,4},{6,5},{7,6},{8,7},{9,8},{10,9},{11,1... | collective-permute-start | bytes 393224 | tf_op jit(solution)/shard_map/ppermute | solution.py:19
  298.6 21.9 %collective-permute-done.2 = f32[2,1,128,128]{3,2,1,0:T(8,128)S(1)} collective-permute-done((f32[2,1,128,128]{3,2,1,0:T(8,128)S(1)}, f32[2,1,128,128]{3,2,1,0:T(8,128)S(1)}, u32[]{:S(2)}, u32[]{:S(2)}) %collective-permute-start.2) | collective-permute-done | bytes 131104 | tf_op jit(solution)/shard_map/ppermute | solution.py:19
  321.1 1.9 collective-permute-start.3
  323.1 1.1 reduce_sum.116
  324.2 16.7 %collective-permute-done.3 = f32[2,1,128,128]{3,2,1,0:T(8,128)S(1)} collective-permute-done((f32[2,1,128,128]{3,2,1,0:T(8,128)S(1)}, f32[2,1,128,128]{3,2,1,0:T(8,128)S(1)}, u32[]{:S(2)}, u32[]{:S(2)}) %collective-permute-start.3) | collective-permute-done | bytes 131104 | tf_op jit(solution)/shard_map/ppermute | solution.py:19
  (60 shorter events, 8.2 us)
Async XLA Ops:
  0.3 0.8 copy-start.6
  21.8 1.0 copy-start.2
  24.8 13.6 %copy-start.7 = (s32[2,128,4]{1,2,0:T(4,128)S(1)}, s32[2,128,4]{1,2,0:T(4,128)}, u32[]{:S(2)}) copy-start(s32[2,128,4]{1,2,0:T(4,128)} %param.6) | copy-start | bytes 12292
  24.8 33.1 %all-to-all-start = ((bf16[2,2,4,128,128]{4,2,0,1,3:T(4,128)(2,1)}), bf16[2,2,4,128,128]{4,2,0,1,3:T(4,128)(2,1)S(1)}, u32[]{:S(2)}, u32[]{:S(2)}) async-start(bf16[2,2,4,128,128]{4,2,0,1,3:T(4,128)(2,1)} %copy.77), calls=%async_computation | async-start | bytes 1048576 | tf_op jit(solution)/shard_map/all_to_all | solution.py:62
  57.9 1.0 copy-start.4
  96.8 61.7 %all-to-all-start.2 = ((f32[16,2,4,8,128]{4,3,2,1,0:T(8,128)}), f32[16,2,4,8,128]{4,3,2,1,0:T(8,128)}, u32[]{:S(2)}, u32[]{:S(2)}) async-start(f32[16,2,4,8,128]{4,3,2,1,0:T(8,128)} %copy.92), calls=%async_computation.2 | async-start | bytes 1048576 | tf_op jit(solution)/shard_map/all_to_all | solution.py:29
  122.8 33.0 %collective-permute-start = (f32[2,1,128,128]{3,2,1,0:T(8,128)S(1)}, f32[2,1,128,128]{3,2,1,0:T(8,128)S(1)}, u32[]{:S(2)}, u32[]{:S(2)}) collective-permute-start(f32[2,1,128,128]{3,2,1,0:T(8,128)S(1)} %slice.135), channel_id=1, source_target_pairs={{1,0},{2,1},{3,2},{4,3},{5,4},{6,5},{7,6},{8,7},{9,8},{10,9},{11,1... | collective-permute-start | bytes 393224 | tf_op jit(solution)/shard_map/ppermute | solution.py:19
  156.5 21.0 %collective-permute-start.1 = (f32[2,1,128,128]{3,2,1,0:T(8,128)S(1)}, f32[2,1,128,128]{3,2,1,0:T(8,128)S(1)}, u32[]{:S(2)}, u32[]{:S(2)}) collective-permute-start(f32[2,1,128,128]{3,2,1,0:T(8,128)S(1)} %slice.140), channel_id=1, source_target_pairs={{0,1},{1,2},{2,3},{3,4},{4,5},{5,6},{6,7},{7,8},{8,9},{9,10},{10,1... | collective-permute-start | bytes 393224 | tf_op jit(solution)/shard_map/ppermute | solution.py:19
  193.4 105.0 %copy-start = (f32[2,4,128,128]{3,2,1,0:T(8,128)}, f32[2,4,128,128]{3,2,1,0:T(8,128)S(1)}, u32[]{:S(2)}) copy-start(f32[2,4,128,128]{3,2,1,0:T(8,128)S(1)} %all_gather.7) | copy-start | bytes 1572868
  198.3 36.2 %copy-start.3 = (f32[2,2,128,4,128]{4,2,3,0,1:T(8,128)S(1)}, f32[2,2,128,4,128]{4,2,3,0,1:T(8,128)}, u32[]{:S(2)}) copy-start(f32[2,2,128,4,128]{4,2,3,0,1:T(8,128)} %get-tuple-element.34) | copy-start | bytes 3145732
  234.3 1.0 copy-start.5
  268.7 54.4 %all-to-all-start.5 = ((f32[16,2,4,8,128]{4,3,2,1,0:T(8,128)}), f32[16,2,4,8,128]{4,3,2,1,0:T(8,128)}, u32[]{:S(2)}, u32[]{:S(2)}) async-start(f32[16,2,4,8,128]{4,3,2,1,0:T(8,128)} %copy.109), calls=%async_computation.5 | async-start | bytes 1048576 | tf_op jit(solution)/shard_map/all_to_all | solution.py:29
  287.5 33.0 %collective-permute-start.2 = (f32[2,1,128,128]{3,2,1,0:T(8,128)S(1)}, f32[2,1,128,128]{3,2,1,0:T(8,128)S(1)}, u32[]{:S(2)}, u32[]{:S(2)}) collective-permute-start(f32[2,1,128,128]{3,2,1,0:T(8,128)S(1)} %slice.149), channel_id=1, source_target_pairs={{1,0},{2,1},{3,2},{4,3},{5,4},{6,5},{7,6},{8,7},{9,8},{10,9},{11,1... | collective-permute-start | bytes 393224 | tf_op jit(solution)/shard_map/ppermute | solution.py:19
  298.5 22.0 %copy-start.1 = (f32[2,4,128,128]{3,2,1,0:T(8,128)S(1)}, f32[2,4,128,128]{3,2,1,0:T(8,128)}, u32[]{:S(2)}) copy-start(f32[2,4,128,128]{3,2,1,0:T(8,128)} %copy-done) | copy-start | bytes 1572868
  298.5 22.0 %slice-start = ((f32[2,4,128,128]{3,2,1,0:T(8,128)}), f32[2,3,128,128]{3,2,1,0:T(8,128)S(1)}, s32[]{:S(2)}) async-start(f32[2,4,128,128]{3,2,1,0:T(8,128)} %copy-done), calls=%async_computation.6 | async-start | bytes 786432 | tf_op jit(solution)/shard_map/slice | solution.py:96
  321.1 19.7 %collective-permute-start.3 = (f32[2,1,128,128]{3,2,1,0:T(8,128)S(1)}, f32[2,1,128,128]{3,2,1,0:T(8,128)S(1)}, u32[]{:S(2)}, u32[]{:S(2)}) collective-permute-start(f32[2,1,128,128]{3,2,1,0:T(8,128)S(1)} %slice.154), channel_id=1, source_target_pairs={{0,1},{1,2},{2,3},{3,4},{4,5},{5,6},{6,7},{7,8},{8,9},{9,10},{10,1... | collective-permute-start | bytes 393224 | tf_op jit(solution)/shard_map/ppermute | solution.py:19
where the time goes:
time: 343 us; the launch traced here: 342 us
  blocking collectives  133 us (39%)
  waiting for transfers between devices  99.5 us (29%)
  starting transfers between devices  81.9 us (24%)
  local copies, waits for them, and re-layouts  10.3 us (3%)
  other arithmetic  8.42 us (2%)
  matrix products  8.42 us (2%)
    ppermute x4, waiting for transfers between devices, from_behind(): return lax.ppermute(block, axis, route)  80.1 us
    all_to_all x2, blocking collectives, data_term(): lax.all_to_all(back_field, 'slab', split_axis=2, concat_axis=3, tiled=True)  60.1 us
    all_to_all x2, starting transfers between devices, sum_at_owner(): lax.all_to_all(tiles, axis, split_axis=0, concat_axis=0, tiled=True)  44.8 us
    all_gather x2, blocking collectives, on_device(): whole_guess = lax.all_gather(guess, 'coil', axis=2, tiled=True)  36.5 us
    all_to_all x1, blocking collectives, data_term(): lax.all_to_all(pieces, 'slab', split_axis=3, concat_axis=2, tiled=True)  35.9 us
    ppermute x4, starting transfers between devices, from_behind(): return lax.ppermute(block, axis, route)  23.5 us
    all_to_all x1, waiting for transfers between devices, data_term(): lax.all_to_all(pieces, 'slab', split_axis=3, concat_axis=2, tiled=True)  19.4 us
    all_to_all x1, starting transfers between devices, data_term(): lax.all_to_all(pieces, 'slab', split_axis=3, concat_axis=2, tiled=True)  13.6 us
  transfers between devices with their start and end apart: 7, of which 5 were waited for; matrix products, arithmetic and copies ran while one was open for 1% of the time, Pallas kernels for 0%

commit v1 on v0

--- a/solution.py
+++ b/solution.py
@@ -133,7 +133,9 @@
     guess = current
     duals = None
     for turn_index in range(ITERS):
-        whole_guess = lax.all_gather(guess, "coil", axis=2, tiled=True)
+        whole_guess = jnp.concatenate(
+            lax.all_to_all(jnp.stack([guess] * lax.axis_size("coil")), "coil", 0, 0), axis=2
+        )
         if duals is None:
             duals = (
                 jnp.zeros_like(whole_guess),

time: 343 us -> 375 us (1.093)
  waiting for transfers between devices: 99.5 us -> 148 us
  starting transfers between devices: 81.9 us -> 66.2 us
  blocking collectives: 133 us -> 124 us
  local copies, waits for them, and re-layouts: 10.3 us -> 14.9 us
    all_gather x2 -> x0, blocking collectives: 36.5 us -> none  [on_device(): whole_guess = lax.all_gather(guess, 'coil', axis=2, tiled=True)]
    all_to_all x0 -> x1, blocking collectives: none -> 31.2 us  [on_device(): lax.all_to_all(jnp.stack([guess] * lax.axis_size('coil')), 'coil', 0, 0)]
    all_to_all x0 -> x1, waiting for transfers between devices: none -> 23.6 us  [on_device(): lax.all_to_all(jnp.stack([guess] * lax.axis_size('coil')), 'coil', 0, 0)]
    all_to_all x2, starting transfers between devices: 44.8 us -> 28.1 us  [sum_at_owner(): lax.all_to_all(tiles, axis, split_axis=0, concat_axis=0, tiled=True)]
    all_to_all x1, waiting for transfers between devices: 19.4 us -> 32.2 us  [data_term(): lax.all_to_all(pieces, 'slab', split_axis=3, concat_axis=2, tiled=True)]
    ppermute x4, waiting for transfers between devices: 80.1 us -> 92.5 us  [from_behind(): return lax.ppermute(block, axis, route)]
    all_to_all x0 -> x1, starting transfers between devices: none -> 11.3 us  [on_device(): lax.all_to_all(jnp.stack([guess] * lax.axis_size('coil')), 'coil', 0, 0)]
    ppermute x4, starting transfers between devices: 23.5 us -> 13.3 us  [from_behind(): return lax.ppermute(block, axis, route)]
  transfers between devices with their start and end apart: 7 -> 8, of which waited for: 5 -> 6; matrix products, arithmetic and copies ran while one was open for 1% -> 2% of each run, Pallas kernels for 0% -> 0%
where the time goes in v1:
time: 375 us; the launch traced here: 374 us
  waiting for transfers between devices  148 us (39%)
  blocking collectives  124 us (33%)
  starting transfers between devices  66.2 us (18%)
  local copies, waits for them, and re-layouts  14.9 us (4%)
  other arithmetic  11.4 us (3%)
  matrix products  8.69 us (2%)
    ppermute x4, waiting for transfers between devices, from_behind(): return lax.ppermute(block, axis, route)  92.5 us
    all_to_all x2, blocking collectives, data_term(): lax.all_to_all(back_field, 'slab', split_axis=2, concat_axis=3, tiled=True)  57 us
    all_to_all x1, blocking collectives, data_term(): lax.all_to_all(pieces, 'slab', split_axis=3, concat_axis=2, tiled=True)  35.8 us
    all_to_all x1, waiting for transfers between devices, data_term(): lax.all_to_all(pieces, 'slab', split_axis=3, concat_axis=2, tiled=True)  32.2 us
    all_to_all x1, blocking collectives, on_device(): lax.all_to_all(jnp.stack([guess] * lax.axis_size('coil')), 'coil', 0, 0)  31.2 us
    all_to_all x2, starting transfers between devices, sum_at_owner(): lax.all_to_all(tiles, axis, split_axis=0, concat_axis=0, tiled=True)  28.1 us
    all_to_all x1, waiting for transfers between devices, on_device(): lax.all_to_all(jnp.stack([guess] * lax.axis_size('coil')), 'coil', 0, 0)  23.6 us
    all_to_all x1, starting transfers between devices, data_term(): lax.all_to_all(pieces, 'slab', split_axis=3, concat_axis=2, tiled=True)  13.5 us
  transfers between devices with their start and end apart: 8, of which 6 were waited for; matrix products, arithmetic and copies ran while one was open for 2% of the time, Pallas kernels for 0%

profile of v1, /device:TPU:130, one launch (start us, length us, event | category | flops | bytes accessed | tf_op | source)
XLA Modules:
  0.0 374.1 jit_solution(3714179130609600074)
XLA Ops:
  0.0 1.6 stack.62
  1.6 11.3 %all-to-all-start = ((f32[16,2,4,8,128]{4,3,2,1,0:T(8,128)}), f32[16,2,4,8,128]{4,3,2,1,0:T(8,128)S(1)}, u32[]{:S(2)}, u32[]{:S(2)}) async-start(f32[16,2,4,8,128]{4,3,2,1,0:T(8,128)} %stack.62), calls=%async_computation | async-start | bytes 1048576 | tf_op jit(solution)/shard_map/all_to_all | solution.py:137
  13.5 23.6 %all-to-all-done = f32[16,2,4,8,128]{4,3,2,1,0:T(8,128)S(1)} async-done(((f32[16,2,4,8,128]{4,3,2,1,0:T(8,128)}), f32[16,2,4,8,128]{4,3,2,1,0:T(8,128)S(1)}, u32[]{:S(2)}, u32[]{:S(2)}) %all-to-all-start) | async-done | bytes 524320 | tf_op jit(solution)/shard_map/all_to_all | solution.py:137
  37.2 1.0 copy-done
  39.0 1.2 copy.82
  40.2 13.5 %all-to-all-start.1 = ((bf16[2,2,4,128,128]{4,2,0,1,3:T(4,128)(2,1)}), bf16[2,2,4,128,128]{4,2,0,1,3:T(4,128)(2,1)S(1)}, u32[]{:S(2)}, u32[]{:S(2)}) async-start(bf16[2,2,4,128,128]{4,2,0,1,3:T(4,128)(2,1)} %copy.82), calls=%async_computation.1 | async-start | bytes 1048576 | tf_op jit(solution)/shard_map/all_to_all | solution.py:62
  53.7 32.2 %all-to-all-done.1 = bf16[2,2,4,128,128]{4,2,0,1,3:T(4,128)(2,1)S(1)} async-done(((bf16[2,2,4,128,128]{4,2,0,1,3:T(4,128)(2,1)}), bf16[2,2,4,128,128]{4,2,0,1,3:T(4,128)(2,1)S(1)}, u32[]{:S(2)}, u32[]{:S(2)}) %all-to-all-start.1) | async-done | bytes 524320 | tf_op jit(solution)/shard_map/all_to_all | solution.py:62
  86.9 1.3 fusion.130
  89.0 28.5 %all_to_all.92 = bf16[2,2,128,4,128]{4,3,0,1,2:T(4,128)(2,1)S(1)} all-to-all(bf16[2,2,128,4,128]{4,3,0,1,2:T(4,128)(2,1)S(1)} %copy.87), channel_id=1, replica_groups=mesh['coil'=16,'slab'=32] {'slab'}, dimensions={2} | all-to-all | bytes 1048576 | tf_op jit(solution)/shard_map/all_to_all | solution.py:78
  119.4 14.0 %all-to-all-start.3 = ((f32[16,2,4,8,128]{4,3,2,1,0:T(8,128)}), f32[16,2,4,8,128]{4,3,2,1,0:T(8,128)S(1)}, u32[]{:S(2)}, u32[]{:S(2)}) async-start(f32[16,2,4,8,128]{4,3,2,1,0:T(8,128)} %copy.97), calls=%async_computation.3 | async-start | bytes 1048576 | tf_op jit(solution)/shard_map/all_to_all | solution.py:29
  133.4 4.7 %collective-permute-start = (f32[2,1,128,128]{3,2,1,0:T(8,128)S(1)}, f32[2,1,128,128]{3,2,1,0:T(8,128)S(1)}, u32[]{:S(2)}, u32[]{:S(2)}) collective-permute-start(f32[2,1,128,128]{3,2,1,0:T(8,128)S(1)} %slice.139), channel_id=1, source_target_pairs={{1,0},{2,1},{3,2},{4,3},{5,4},{6,5},{7,6},{8,7},{9,8},{10,9},{11,1... | collective-permute-start | bytes 393224 | tf_op jit(solution)/shard_map/ppermute | solution.py:19
  138.6 27.6 %collective-permute-done = f32[2,1,128,128]{3,2,1,0:T(8,128)S(1)} collective-permute-done((f32[2,1,128,128]{3,2,1,0:T(8,128)S(1)}, f32[2,1,128,128]{3,2,1,0:T(8,128)S(1)}, u32[]{:S(2)}, u32[]{:S(2)}) %collective-permute-start) | collective-permute-done | bytes 131104 | tf_op jit(solution)/shard_map/ppermute | solution.py:19
  168.2 1.9 collective-permute-start.1
  171.5 19.5 %collective-permute-done.1 = f32[2,1,128,128]{3,2,1,0:T(8,128)} collective-permute-done((f32[2,1,128,128]{3,2,1,0:T(8,128)}, f32[2,1,128,128]{3,2,1,0:T(8,128)}, u32[]{:S(2)}, u32[]{:S(2)}) %collective-permute-start.1) | collective-permute-done | bytes 131104 | tf_op jit(solution)/shard_map/ppermute | solution.py:19
  191.0 1.5 multiply_subtract_fusion.1
  192.5 31.2 %all_to_all.93 = f32[16,2,4,8,128]{4,3,2,1,0:T(8,128)S(1)} all-to-all(f32[16,2,4,8,128]{4,3,2,1,0:T(8,128)S(1)} %stack.67), channel_id=1, replica_groups=mesh['coil'=16,'slab'=32] {'coil'}, dimensions={0} | all-to-all | bytes 1048576 | tf_op jit(solution)/shard_map/all_to_all | solution.py:137
  223.9 1.0 fusion.32
  224.9 2.6 fusion.18
  227.4 1.4 copy.100
  228.9 35.8 %all_to_all.94 = bf16[2,2,4,128,128]{4,2,0,1,3:T(4,128)(2,1)S(1)} all-to-all(bf16[2,2,4,128,128]{4,2,0,1,3:T(4,128)(2,1)S(1)} %copy.100), channel_id=1, replica_groups=mesh['coil'=16,'slab'=32] {'slab'}, dimensions={3} | all-to-all | bytes 1048576 | tf_op jit(solution)/shard_map/all_to_all | solution.py:62
  267.3 28.5 %all_to_all.95 = bf16[2,2,128,4,128]{4,3,0,1,2:T(4,128)(2,1)S(1)} all-to-all(bf16[2,2,128,4,128]{4,3,0,1,2:T(4,128)(2,1)S(1)} %copy.105), channel_id=1, replica_groups=mesh['coil'=16,'slab'=32] {'slab'}, dimensions={2} | all-to-all | bytes 1048576 | tf_op jit(solution)/shard_map/all_to_all | solution.py:78
  295.8 1.1 copy.106
  296.9 2.7 convolution_bitcast_fusion
  299.6 1.4 fusion.36
  301.9 14.1 %all-to-all-start.7 = ((f32[16,2,4,8,128]{4,3,2,1,0:T(8,128)}), f32[16,2,4,8,128]{4,3,2,1,0:T(8,128)}, u32[]{:S(2)}, u32[]{:S(2)}) async-start(f32[16,2,4,8,128]{4,3,2,1,0:T(8,128)} %copy.115), calls=%async_computation.7 | async-start | bytes 1048576 | tf_op jit(solution)/shard_map/all_to_all | solution.py:29
  316.1 1.1 fusion.82
  317.2 4.7 %collective-permute-start.2 = (f32[2,1,128,128]{3,2,1,0:T(8,128)S(1)}, f32[2,1,128,128]{3,2,1,0:T(8,128)S(1)}, u32[]{:S(2)}, u32[]{:S(2)}) collective-permute-start(f32[2,1,128,128]{3,2,1,0:T(8,128)S(1)} %slice.153), channel_id=1, source_target_pairs={{1,0},{2,1},{3,2},{4,3},{5,4},{6,5},{7,6},{8,7},{9,8},{10,9},{11,1... | collective-permute-start | bytes 393224 | tf_op jit(solution)/shard_map/ppermute | solution.py:19
  322.4 26.5 %collective-permute-done.2 = f32[2,1,128,128]{3,2,1,0:T(8,128)S(1)} collective-permute-done((f32[2,1,128,128]{3,2,1,0:T(8,128)S(1)}, f32[2,1,128,128]{3,2,1,0:T(8,128)S(1)}, u32[]{:S(2)}, u32[]{:S(2)}) %collective-permute-start.2) | collective-permute-done | bytes 131104 | tf_op jit(solution)/shard_map/ppermute | solution.py:19
  350.2 1.1 fusion.53
  351.4 2.1 collective-permute-start.3
  353.5 1.1 reduce_sum.125
  354.6 18.8 %collective-permute-done.3 = f32[2,1,128,128]{3,2,1,0:T(8,128)S(1)} collective-permute-done((f32[2,1,128,128]{3,2,1,0:T(8,128)S(1)}, f32[2,1,128,128]{3,2,1,0:T(8,128)S(1)}, u32[]{:S(2)}, u32[]{:S(2)}) %collective-permute-start.3) | collective-permute-done | bytes 131104 | tf_op jit(solution)/shard_map/ppermute | solution.py:19
  (97 shorter events, 14.9 us)
Async XLA Ops:
  1.6 35.5 %all-to-all-start = ((f32[16,2,4,8,128]{4,3,2,1,0:T(8,128)}), f32[16,2,4,8,128]{4,3,2,1,0:T(8,128)S(1)}, u32[]{:S(2)}, u32[]{:S(2)}) async-start(f32[16,2,4,8,128]{4,3,2,1,0:T(8,128)} %stack.62), calls=%async_computation | async-start | bytes 1048576 | tf_op jit(solution)/shard_map/all_to_all | solution.py:137
  13.5 72.7 %copy-start.18 = (bf16[1,2,128,128]{2,3,0,1:T(8,128)(2,1)}, bf16[1,2,128,128]{2,3,0,1:T(8,128)(2,1)S(1)}, u32[]{:S(2)}) copy-start(bf16[1,2,128,128]{2,3,0,1:T(8,128)(2,1)S(1)} %get-tuple-element.34) | copy-start | bytes 196612
  13.5 72.7 %copy-start.20 = (bf16[1,2,128,128]{2,3,0,1:T(8,128)(2,1)}, bf16[1,2,128,128]{2,3,0,1:T(8,128)(2,1)S(1)}, u32[]{:S(2)}) copy-start(bf16[1,2,128,128]{2,3,0,1:T(8,128)(2,1)S(1)} %get-tuple-element.37) | copy-start | bytes 196612
  13.5 104.3 %copy-start.3 = (bf16[1,2,128,128]{2,3,1,0:T(8,128)(2,1)}, bf16[1,2,128,128]{2,3,1,0:T(8,128)(2,1)S(1)}, u32[]{:S(2)}) copy-start(bf16[1,2,128,128]{2,3,1,0:T(8,128)(2,1)S(1)} %get-tuple-element.33) | copy-start | bytes 196612
  13.5 104.3 %copy-start.5 = (bf16[1,2,128,128]{2,3,1,0:T(8,128)(2,1)}, bf16[1,2,128,128]{2,3,1,0:T(8,128)(2,1)S(1)}, u32[]{:S(2)}) copy-start(bf16[1,2,128,128]{2,3,1,0:T(8,128)(2,1)S(1)} %get-tuple-element.38) | copy-start | bytes 196612
  37.2 1.0 copy-start
  40.2 13.5 %copy-start.23 = (s32[2,128,4]{1,2,0:T(4,128)S(1)}, s32[2,128,4]{1,2,0:T(4,128)}, u32[]{:S(2)}) copy-start(s32[2,128,4]{1,2,0:T(4,128)} %param.6) | copy-start | bytes 12292
  40.2 45.7 %all-to-all-start.1 = ((bf16[2,2,4,128,128]{4,2,0,1,3:T(4,128)(2,1)}), bf16[2,2,4,128,128]{4,2,0,1,3:T(4,128)(2,1)S(1)}, u32[]{:S(2)}, u32[]{:S(2)}) async-start(bf16[2,2,4,128,128]{4,2,0,1,3:T(4,128)(2,1)} %copy.82), calls=%async_computation.1 | async-start | bytes 1048576 | tf_op jit(solution)/shard_map/all_to_all | solution.py:62
  85.9 1.0 copy-start.16
  119.4 51.5 %all-to-all-start.3 = ((f32[16,2,4,8,128]{4,3,2,1,0:T(8,128)}), f32[16,2,4,8,128]{4,3,2,1,0:T(8,128)S(1)}, u32[]{:S(2)}, u32[]{:S(2)}) async-start(f32[16,2,4,8,128]{4,3,2,1,0:T(8,128)} %copy.97), calls=%async_computation.3 | async-start | bytes 1048576 | tf_op jit(solution)/shard_map/all_to_all | solution.py:29
  133.4 32.8 %collective-permute-start = (f32[2,1,128,128]{3,2,1,0:T(8,128)S(1)}, f32[2,1,128,128]{3,2,1,0:T(8,128)S(1)}, u32[]{:S(2)}, u32[]{:S(2)}) collective-permute-start(f32[2,1,128,128]{3,2,1,0:T(8,128)S(1)} %slice.139), channel_id=1, source_target_pairs={{1,0},{2,1},{3,2},{4,3},{5,4},{6,5},{7,6},{8,7},{9,8},{10,9},{11,1... | collective-permute-start | bytes 393224 | tf_op jit(solution)/shard_map/ppermute | solution.py:19
  138.6 27.9 %copy-start.9 = (f32[4,128,128]{2,1,0:T(8,128)}, f32[4,128,128]{2,1,0:T(8,128)S(1)}, u32[]{:S(2)}) copy-start(f32[4,128,128]{2,1,0:T(8,128)S(1)} %get-tuple-element.43) | copy-start | bytes 786436
  138.6 27.9 %copy-start.11 = (f32[4,128,128]{2,1,0:T(8,128)}, f32[4,128,128]{2,1,0:T(8,128)S(1)}, u32[]{:S(2)}) copy-start(f32[4,128,128]{2,1,0:T(8,128)S(1)} %get-tuple-element.44) | copy-start | bytes 786436
  166.2 0.9 copy-start.13
  166.4 0.7 copy-start.7
  167.4 23.6 %copy-start.1 = (f32[2,4,128,128]{3,2,1,0:T(8,128)}, f32[2,4,128,128]{3,2,1,0:T(8,128)S(1)}, u32[]{:S(2)}) copy-start(f32[2,4,128,128]{3,2,1,0:T(8,128)S(1)} %get-tuple-element.30) | copy-start | bytes 1572868
  168.2 22.8 %collective-permute-start.1 = (f32[2,1,128,128]{3,2,1,0:T(8,128)}, f32[2,1,128,128]{3,2,1,0:T(8,128)}, u32[]{:S(2)}, u32[]{:S(2)}) collective-permute-start(f32[2,1,128,128]{3,2,1,0:T(8,128)} %slice.144), channel_id=1, source_target_pairs={{0,1},{1,2},{2,3},{3,4},{4,5},{5,6},{6,7},{7,8},{8,9},{9,10},{10,1... | collective-permute-start | bytes 393224 | tf_op jit(solution)/shard_map/ppermute | solution.py:19
  228.9 36.0 %copy-start.15 = (f32[2,2,128,4,128]{4,2,3,0,1:T(8,128)S(1)}, f32[2,2,128,4,128]{4,2,3,0,1:T(8,128)}, u32[]{:S(2)}) copy-start(f32[2,2,128,4,128]{4,2,3,0,1:T(8,128)} %get-tuple-element.40) | copy-start | bytes 3145732
  264.7 1.0 copy-start.17
  264.7 1.0 copy-start.19
  264.7 1.0 copy-start.21
  265.7 0.8 copy-start.4
  265.7 0.9 copy-start.6
  301.9 14.1 %copy-start.8 = (f32[4,16,8,128]{3,2,1,0:T(8,128)S(1)}, f32[4,16,8,128]{3,2,1,0:T(8,128)}, u32[]{:S(2)}) copy-start(f32[4,16,8,128]{3,2,1,0:T(8,128)} %copy-done.7) | copy-start | bytes 786436
  301.9 14.1 %copy-start.10 = (f32[4,128,128]{2,1,0:T(8,128)S(1)}, f32[4,128,128]{2,1,0:T(8,128)}, u32[]{:S(2)}) copy-start(f32[4,128,128]{2,1,0:T(8,128)} %copy-done.9) | copy-start | bytes 786436
  301.9 51.6 %all-to-all-start.7 = ((f32[16,2,4,8,128]{4,3,2,1,0:T(8,128)}), f32[16,2,4,8,128]{4,3,2,1,0:T(8,128)}, u32[]{:S(2)}, u32[]{:S(2)}) async-start(f32[16,2,4,8,128]{4,3,2,1,0:T(8,128)} %copy.115), calls=%async_computation.7 | async-start | bytes 1048576 | tf_op jit(solution)/shard_map/all_to_all | solution.py:29
  317.2 31.7 %collective-permute-start.2 = (f32[2,1,128,128]{3,2,1,0:T(8,128)S(1)}, f32[2,1,128,128]{3,2,1,0:T(8,128)S(1)}, u32[]{:S(2)}, u32[]{:S(2)}) collective-permute-start(f32[2,1,128,128]{3,2,1,0:T(8,128)S(1)} %slice.153), channel_id=1, source_target_pairs={{1,0},{2,1},{3,2},{4,3},{5,4},{6,5},{7,6},{8,7},{9,8},{10,9},{11,1... | collective-permute-start | bytes 393224 | tf_op jit(solution)/shard_map/ppermute | solution.py:19
  322.3 26.6 %copy-start.14 = (f32[2,1,128,128]{3,2,1,0:T(8,128)S(1)}, f32[2,1,128,128]{3,2,1,0:T(8,128)}, u32[]{:S(2)}) copy-start(f32[2,1,128,128]{3,2,1,0:T(8,128)} %copy-done.13) | copy-start | bytes 393220
  349.1 1.0 copy-start.2
  351.3 22.1 %copy-start.12 = (f32[2,4,128,128]{3,2,1,0:T(8,128)S(1)}, f32[2,4,128,128]{3,2,1,0:T(8,128)}, u32[]{:S(2)}) copy-start(f32[2,4,128,128]{3,2,1,0:T(8,128)} %get-tuple-element.29) | copy-start | bytes 1572868
  351.4 22.0 %collective-permute-start.3 = (f32[2,1,128,128]{3,2,1,0:T(8,128)S(1)}, f32[2,1,128,128]{3,2,1,0:T(8,128)S(1)}, u32[]{:S(2)}, u32[]{:S(2)}) collective-permute-start(f32[2,1,128,128]{3,2,1,0:T(8,128)S(1)} %slice.158), channel_id=1, source_target_pairs={{0,1},{1,2},{2,3},{3,4},{4,5},{5,6},{6,7},{7,8},{8,9},{9,10},{10,1... | collective-permute-start | bytes 393224 | tf_op jit(solution)/shard_map/ppermute | solution.py:19
  353.4 20.0 %copy-start.22 = (f32[2,4,8,128]{3,2,1,0:T(8,128)S(1)}, f32[2,4,8,128]{3,2,1,0:T(8,128)}, u32[]{:S(2)}) copy-start(f32[2,4,8,128]{3,2,1,0:T(8,128)} %get-tuple-element.10) | copy-start | bytes 98308
